TPU v7x, 32 devices: a whole 2x2x4 slice. The times are simulated.
32 devices in a mesh: dp: 4 (over z), expert: 8 (over y, x, core).
Axes of the slice: x: 2, y: 2, z: 4, core: 2. Of those that a mesh axis runs over, the one named last changes fastest.
Arguments:
- tokens: bfloat16 [16384, 768], P(('dp', 'expert')), may hold values from -6 to 6
- lengths: int32 [64, 3], P(('dp', 'expert')), may hold values from 1 to 128, 256 in all within a row
- routes: int32 [2, 16384, 1], P(None, ('dp', 'expert')), may hold values from 0 to 7; in each aligned block of 256 rows (0 to 255, 256 to 511, ..., all dimensions but the last counted through in order) at most 64 rows name the same one
- qkv_weights: bfloat16 [3538944], P(('dp', 'expert')), may hold values from -0.21875 to 0.21875
- out_weights: bfloat16 [1179648], P(('dp', 'expert')), may hold values from -0.875 to 0.875
- gains: bfloat16 [3072], P(('dp', 'expert')), may hold values from 0.099609375 to 1.8984375
- bias_table: bfloat16 [768], P(('dp', 'expert')), may hold values from -4 to 4
- router: bfloat16 [12288], P(('dp', 'expert')), may hold values from -0.15625 to 0.15625
- expert_in: bfloat16 [2, 8, 768, 3072], P(None, 'expert', None, 'dp'), may hold values from -0.21875 to 0.21875
- expert_out: bfloat16 [2, 8, 3072, 768], P(None, 'expert', 'dp'), may hold values from -1.25 to 1.25
- cotangent: bfloat16 [16384, 768], P(('dp', 'expert')), may hold values from -6 to 6
Outputs:
- mixed: bfloat16 [16384, 768], P(('dp', 'expert'))
- input_grad: float32 [16384, 768], P(('dp', 'expert'))
- qkv_grad: float32 [3538944], P(('dp', 'expert'))
- out_grad: float32 [1179648], P(('dp', 'expert'))
- gains_grad: float32 [3072], P(('dp', 'expert'))
- table_grad: float32 [768], P(('dp', 'expert'))
- router_grad: float32 [12288], P(('dp', 'expert'))
- expert_in_grad: float32 [2, 8, 768, 3072], P(None, 'expert', None, 'dp')
- expert_out_grad: float32 [2, 8, 3072, 768], P(None, 'expert', 'dp')
Inputs may be any that keep to these rules, and one draw needn't show every extreme that they name: Each row holds the lengths of one micro-batch's sequences, summing to 256; the longest is exactly half of 256. `routes`: within each micro-batch of one device (aligned blocks of 256 tokens of one layer) no expert is named by more than 64 tokens, a bound that some block reaches.
All inputs are finite; a program needn't handle non-finite values.
Results may differ from a plain program's by a relative error of at most 0.035.
Values may be sent and summed in bfloat16 or wider, within the bound.
A program may use at most 320 MiB of HBM per device.

v0:
```python
import jax
import jax.numpy as jnp
from jax import lax
from jax.sharding import PartitionSpec as P

H = 12
FF = 3072
NB = 32
LAYERS = 2


eps_norm = 1e-06
score_scale = 0.125
masked_score = -1e30
bucket_edges = (1, 2, 3, 4, 5, 6, 7, 8, 12, 16, 23, 32, 45, 64, 91)


def bucket_table(row_count, bucket_count):
    places = jnp.arange(row_count, dtype=jnp.int32)
    offset = places[None, :] - places[:, None]
    distance = jnp.abs(offset)
    bucket = jnp.zeros((row_count, row_count), jnp.int32)
    for edge in bucket_edges:
        bucket = bucket + (distance >= edge).astype(jnp.int32)
    bucket = bucket + bucket_count // 2 * (offset > 0).astype(jnp.int32)
    return (bucket[:, :, None] == jnp.arange(bucket_count, dtype=jnp.int32)[None, None, :]).astype(
        jnp.bfloat16
    )


def same_sequence(seq_lengths, row_count):
    ends = jnp.cumsum(seq_lengths)
    places = jnp.arange(row_count, dtype=jnp.int32)
    segment = jnp.sum((places[:, None] >= ends[None, :]).astype(jnp.int32), axis=1)
    return segment[:, None] == segment[None, :]


def unit_scale(stream):
    recip = lax.rsqrt(jnp.mean(stream * stream, axis=-1, keepdims=True) + eps_norm)
    return (stream * recip, recip)


def norm_back(grad_normed, unit_rows, recip, gain_row):
    grad_unit = grad_normed * gain_row
    grad_stream = recip * (
        grad_unit - unit_rows * jnp.mean(grad_unit * unit_rows, axis=-1, keepdims=True)
    )
    return (grad_stream, jnp.sum(grad_normed * unit_rows, axis=0))


def softmax_rows(scores):
    row_top = jnp.max(scores, axis=-1, keepdims=True)
    exp_terms = jnp.exp(scores - row_top)
    return exp_terms / jnp.sum(exp_terms, axis=-1, keepdims=True)


def dispatch_table(route_ids, expert_count, capacity):
    chosen = (route_ids == jnp.arange(expert_count, dtype=jnp.int32)[None, :]).astype(jnp.int32)
    position = jnp.sum(jnp.cumsum(chosen, axis=0) * chosen, axis=1) - 1
    slot_hit = (position[:, None] == jnp.arange(capacity, dtype=jnp.int32)[None, :]).astype(
        jnp.bfloat16
    )
    onehot = chosen.astype(jnp.bfloat16)
    return (chosen.astype(jnp.float32), onehot[:, :, None] * slot_hit[:, None, :])


def masked_scores(split_heads, rel_bias, allowed):
    raw = jnp.einsum(
        "ihd,jhd->hij", split_heads[0], split_heads[1], preferred_element_type=jnp.float32
    )
    return jnp.where(allowed[None], raw * score_scale + rel_bias, masked_score)


def attend_forward(normed, weights_qkv, rel_bias, allowed):
    row_count = normed.shape[0]
    projected = jnp.einsum(
        "td,kde->kte", normed, weights_qkv, preferred_element_type=jnp.float32
    ).astype(jnp.bfloat16)
    split_heads = projected.reshape(3, row_count, H, -1)
    scores = masked_scores(split_heads, rel_bias, allowed)
    row_top = jnp.max(scores, axis=-1, keepdims=True)
    exp_terms = jnp.exp(scores - row_top)
    row_total = jnp.sum(exp_terms, axis=-1, keepdims=True)
    attn_probs = (exp_terms / row_total).astype(jnp.bfloat16)
    attended = jnp.einsum(
        "hij,jhd->ihd", attn_probs, split_heads[2], preferred_element_type=jnp.float32
    )
    attended = attended.reshape(row_count, -1).astype(jnp.bfloat16)
    return (projected, attended, row_top + jnp.log(row_total))


def attend_backward(
    grad_attended, normed, projected, rel_bias, allowed, log_total, weights_qkv, bucket_onehot
):
    row_count = normed.shape[0]
    split_heads = projected.reshape(3, row_count, H, -1)
    grad_heads = grad_attended.reshape(row_count, H, -1)
    attn_probs = jnp.exp(masked_scores(split_heads, rel_bias, allowed) - log_total)
    grad_values = jnp.einsum(
        "hij,ihd->jhd",
        attn_probs.astype(jnp.bfloat16),
        grad_heads,
        preferred_element_type=jnp.float32,
    )
    grad_probs = jnp.einsum(
        "ihd,jhd->hij", grad_heads, split_heads[2], preferred_element_type=jnp.float32
    )
    row_delta = jnp.sum(attn_probs * grad_probs, axis=-1, keepdims=True)
    grad_scores = (attn_probs * (grad_probs - row_delta)).astype(jnp.bfloat16)
    grad_query = (
        jnp.einsum("hij,jhd->ihd", grad_scores, split_heads[1], preferred_element_type=jnp.float32)
        * score_scale
    )
    grad_keys = (
        jnp.einsum("hij,ihd->jhd", grad_scores, split_heads[0], preferred_element_type=jnp.float32)
        * score_scale
    )
    grad_table = jnp.einsum(
        "hij,ijb->bh", grad_scores, bucket_onehot, preferred_element_type=jnp.float32
    )
    grad_proj = (
        jnp.stack([grad_query, grad_keys, grad_values])
        .reshape(3, row_count, -1)
        .astype(jnp.bfloat16)
    )
    grad_qkv = jnp.einsum("td,kte->kde", normed, grad_proj, preferred_element_type=jnp.float32)
    grad_normed = jnp.einsum(
        "kte,kde->td", grad_proj, weights_qkv, preferred_element_type=jnp.float32
    )
    return (grad_qkv, grad_table, grad_normed)


def per_device(
    tokens,
    lengths,
    routes,
    qkv_weights,
    out_weights,
    gains,
    bias_table,
    router,
    expert_in,
    expert_out,
    cotangent,
):
    micro_count = lengths.shape[0]
    block_rows = tokens.shape[0] // micro_count
    layer_count = LAYERS
    model_width = tokens.shape[1]
    expert_count = expert_in.shape[1] * lax.axis_size("expert")
    full_qkv, full_out, full_gain, full_table, full_router = (
        lax.all_gather(qkv_weights, ("dp", "expert"), axis=0, tiled=True),
        lax.all_gather(out_weights, ("dp", "expert"), axis=0, tiled=True),
        lax.all_gather(gains, ("dp", "expert"), axis=0, tiled=True),
        lax.all_gather(bias_table, ("dp", "expert"), axis=0, tiled=True),
        lax.all_gather(router, ("dp", "expert"), axis=0, tiled=True),
    )
    full_qkv = full_qkv.reshape(layer_count, 3, model_width, model_width)
    full_out = full_out.reshape(layer_count, model_width, model_width)
    full_gain = full_gain.reshape(layer_count, 2, model_width)
    full_router = full_router.reshape(layer_count, model_width, expert_count)
    bias_rows = full_table.reshape(layer_count, NB, H)
    capacity = 2 * block_rows // expert_count
    bucket_onehot = bucket_table(block_rows, NB)
    saved = []
    mixed_parts = []
    for batch_no in range(micro_count):
        row_start = batch_no * block_rows
        stream = tokens[row_start : row_start + block_rows].astype(jnp.float32)
        allowed = same_sequence(lengths[batch_no], block_rows)
        batch_saved = []
        for layer_no in range(layer_count):
            layer_in, layer_out = (
                lax.all_gather(expert_in[layer_no], "dp", axis=2, tiled=True),
                lax.all_gather(expert_out[layer_no], "dp", axis=1, tiled=True),
            )
            weight_in = layer_in[0]
            weight_out = layer_out[0]
            gain_pair = full_gain[layer_no].astype(jnp.float32)
            rel_bias = jnp.einsum(
                "ijb,bh->hij",
                bucket_onehot,
                bias_rows[layer_no],
                preferred_element_type=jnp.float32,
            )
            unit_one, recip_one = unit_scale(stream)
            normed = (unit_one * gain_pair[0]).astype(jnp.bfloat16)
            projected, attended, log_total = attend_forward(
                normed, full_qkv[layer_no], rel_bias, allowed
            )
            after_attn = stream + jnp.dot(
                attended, full_out[layer_no], preferred_element_type=jnp.float32
            )
            unit_two, recip_two = unit_scale(after_attn)
            normed_two = (unit_two * gain_pair[1]).astype(jnp.bfloat16)
            chance = softmax_rows(
                jnp.dot(normed_two, full_router[layer_no], preferred_element_type=jnp.float32)
            )
            onehot, slot_table = dispatch_table(
                routes[layer_no, row_start : row_start + block_rows], expert_count, capacity
            )
            gate_value = jnp.sum(chance * onehot, axis=1)
            slot_rows = jnp.einsum(
                "tec,td->ecd", slot_table, normed_two, preferred_element_type=jnp.float32
            ).astype(jnp.bfloat16)
            arrived = lax.all_to_all(slot_rows, "expert", split_axis=0, concat_axis=0, tiled=True)
            source_count = arrived.shape[0]
            item_count = arrived.shape[1]
            expert_flat_rows = arrived.reshape(source_count * item_count, model_width)
            inner_act = jnp.dot(expert_flat_rows, weight_in, preferred_element_type=jnp.float32)
            expert_hidden = jax.nn.gelu(inner_act).astype(jnp.bfloat16)
            outer_act = jnp.dot(
                expert_hidden, weight_out, preferred_element_type=jnp.float32
            ).astype(jnp.bfloat16)
            returned = lax.all_to_all(
                outer_act.reshape(source_count, item_count, model_width),
                "expert",
                split_axis=0,
                concat_axis=0,
                tiled=True,
            )
            returned, arrived, inner_act = (
                returned,
                arrived,
                inner_act.reshape(source_count, item_count, -1),
            )
            expert_mix = jnp.einsum(
                "tec,ecd->td", slot_table, returned, preferred_element_type=jnp.float32
            )
            batch_saved.append(
                (
                    stream,
                    after_attn,
                    normed,
                    projected,
                    attended,
                    log_total,
                    normed_two,
                    chance,
                    onehot,
                    slot_table,
                    gate_value,
                    expert_mix,
                    arrived,
                    inner_act,
                )
            )
            stream = after_attn + gate_value[:, None] * expert_mix
        saved.append(batch_saved)
        mixed_parts.append(stream)
    mixed = jnp.concatenate(mixed_parts, axis=0).astype(jnp.bfloat16)
    back_qkv, back_out, back_gain, back_table, back_router = (
        lax.all_gather(qkv_weights, ("dp", "expert"), axis=0, tiled=True),
        lax.all_gather(out_weights, ("dp", "expert"), axis=0, tiled=True),
        lax.all_gather(gains, ("dp", "expert"), axis=0, tiled=True),
        lax.all_gather(bias_table, ("dp", "expert"), axis=0, tiled=True),
        lax.all_gather(router, ("dp", "expert"), axis=0, tiled=True),
    )
    back_qkv = back_qkv.reshape(layer_count, 3, model_width, model_width)
    back_out = back_out.reshape(layer_count, model_width, model_width)
    back_gain = back_gain.reshape(layer_count, 2, model_width)
    back_router = back_router.reshape(layer_count, model_width, expert_count)
    back_rows = back_table.reshape(layer_count, NB, H)
    acc_qkv = [
        jnp.zeros((3, model_width, model_width), jnp.float32) for layer_no in range(layer_count)
    ]
    acc_out = [
        jnp.zeros((model_width, model_width), jnp.float32) for layer_no in range(layer_count)
    ]
    acc_gain = [jnp.zeros((2, model_width), jnp.float32) for layer_no in range(layer_count)]
    acc_table = [jnp.zeros((NB, H), jnp.float32) for layer_no in range(layer_count)]
    acc_router = [
        jnp.zeros((model_width, expert_count), jnp.float32) for layer_no in range(layer_count)
    ]
    acc_ein = [jnp.zeros((model_width, FF), jnp.float32) for layer_no in range(layer_count)]
    acc_eout = [jnp.zeros((FF, model_width), jnp.float32) for layer_no in range(layer_count)]
    grad_parts = []
    for batch_no in range(micro_count):
        row_start = batch_no * block_rows
        allowed = same_sequence(lengths[batch_no], block_rows)
        grad_stream = cotangent[row_start : row_start + block_rows].astype(jnp.float32)
        for layer_no in reversed(range(layer_count)):
            (
                stream,
                after_attn,
                normed,
                projected,
                attended,
                log_total,
                normed_two,
                chance,
                onehot,
                slot_table,
                gate_value,
                expert_mix,
                arrived,
                inner_act,
            ) = saved[batch_no][layer_no]
            layer_in, layer_out = (
                lax.all_gather(expert_in[layer_no], "dp", axis=2, tiled=True),
                lax.all_gather(expert_out[layer_no], "dp", axis=1, tiled=True),
            )
            weight_in = layer_in[0]
            weight_out = layer_out[0]
            gain_pair = back_gain[layer_no].astype(jnp.float32)
            grad_mix = (gate_value[:, None] * grad_stream).astype(jnp.bfloat16)
            grad_gate = jnp.sum(grad_stream * expert_mix, axis=1)
            grad_logits = (
                chance * (grad_gate[:, None] * onehot - (gate_value * grad_gate)[:, None])
            ).astype(jnp.bfloat16)
            acc_router[layer_no] = acc_router[layer_no] + jnp.einsum(
                "td,te->de", normed_two, grad_logits, preferred_element_type=jnp.float32
            )
            grad_normed_two = jnp.einsum(
                "te,de->td", grad_logits, back_router[layer_no], preferred_element_type=jnp.float32
            )
            grad_slots = jnp.einsum(
                "tec,td->ecd", slot_table, grad_mix, preferred_element_type=jnp.float32
            ).astype(jnp.bfloat16)
            arrived_grad = lax.all_to_all(
                grad_slots, "expert", split_axis=0, concat_axis=0, tiled=True
            )
            flat_grad = arrived_grad.reshape(-1, model_width)
            flat_rows = arrived.reshape(-1, model_width)
            flat_inner = inner_act.reshape(flat_grad.shape[0], -1)
            hidden = jax.nn.gelu(flat_inner).astype(jnp.bfloat16)
            acc_eout[layer_no] = acc_eout[layer_no] + jnp.einsum(
                "rf,rd->fd", hidden, flat_grad, preferred_element_type=jnp.float32
            )
            grad_hidden = jnp.einsum(
                "rd,fd->rf", flat_grad, weight_out, preferred_element_type=jnp.float32
            )
            unused, pull_back = jax.vjp(jax.nn.gelu, flat_inner)
            grad_inner = pull_back(grad_hidden)[0].astype(jnp.bfloat16)
            acc_ein[layer_no] = acc_ein[layer_no] + jnp.einsum(
                "rd,rf->df", flat_rows, grad_inner, preferred_element_type=jnp.float32
            )
            grad_rows = jnp.einsum(
                "rf,df->rd", grad_inner, weight_in, preferred_element_type=jnp.float32
            ).astype(jnp.bfloat16)
            grad_back = lax.all_to_all(
                grad_rows.reshape(arrived_grad.shape),
                "expert",
                split_axis=0,
                concat_axis=0,
                tiled=True,
            )
            grad_normed_two = grad_normed_two + jnp.einsum(
                "tec,ecd->td", slot_table, grad_back, preferred_element_type=jnp.float32
            )
            unit_two, recip_two = unit_scale(after_attn)
            grad_after, gain_two = norm_back(grad_normed_two, unit_two, recip_two, gain_pair[1])
            grad_after = grad_stream + grad_after
            grad_branch = grad_after.astype(jnp.bfloat16)
            acc_out[layer_no] = acc_out[layer_no] + jnp.einsum(
                "td,te->de", attended, grad_branch, preferred_element_type=jnp.float32
            )
            grad_attended = jnp.einsum(
                "te,de->td", grad_branch, back_out[layer_no], preferred_element_type=jnp.float32
            ).astype(jnp.bfloat16)
            rel_bias = jnp.einsum(
                "ijb,bh->hij",
                bucket_onehot,
                back_rows[layer_no],
                preferred_element_type=jnp.float32,
            )
            grad_qkv, grad_table, grad_normed = attend_backward(
                grad_attended,
                normed,
                projected,
                rel_bias,
                allowed,
                log_total,
                back_qkv[layer_no],
                bucket_onehot,
            )
            acc_qkv[layer_no] = acc_qkv[layer_no] + grad_qkv
            acc_table[layer_no] = acc_table[layer_no] + grad_table
            unit_one, recip_one = unit_scale(stream)
            grad_input, gain_one = norm_back(grad_normed, unit_one, recip_one, gain_pair[0])
            acc_gain[layer_no] = acc_gain[layer_no] + jnp.stack([gain_one, gain_two])
            grad_stream = grad_after + grad_input
        grad_parts.append(grad_stream)
    input_grad = jnp.concatenate(grad_parts, axis=0)
    param_sums = (
        lax.psum_scatter(
            jnp.stack(acc_qkv).reshape(-1), ("dp", "expert"), scatter_dimension=0, tiled=True
        ),
        lax.psum_scatter(
            jnp.stack(acc_out).reshape(-1), ("dp", "expert"), scatter_dimension=0, tiled=True
        ),
        lax.psum_scatter(
            jnp.stack(acc_gain).reshape(-1), ("dp", "expert"), scatter_dimension=0, tiled=True
        ),
        lax.psum_scatter(
            jnp.stack(acc_table).reshape(-1), ("dp", "expert"), scatter_dimension=0, tiled=True
        ),
        lax.psum_scatter(
            jnp.stack(acc_router).reshape(-1), ("dp", "expert"), scatter_dimension=0, tiled=True
        ),
    )
    expert_sums = (
        lax.psum_scatter(
            jnp.stack(acc_ein)[:, None].astype(jnp.bfloat16), "dp", scatter_dimension=3, tiled=True
        ).astype(jnp.float32),
        lax.psum_scatter(
            jnp.stack(acc_eout)[:, None].astype(jnp.bfloat16), "dp", scatter_dimension=2, tiled=True
        ).astype(jnp.float32),
    )
    return (
        mixed,
        input_grad,
        param_sums[0],
        param_sums[1],
        param_sums[2],
        param_sums[3],
        param_sums[4],
        expert_sums[0],
        expert_sums[1],
    )


def solution(mesh):
    placed = (
        P(("dp", "expert"), None),
        P(("dp", "expert"), None),
        P(None, ("dp", "expert"), None),
        P(("dp", "expert")),
        P(("dp", "expert")),
        P(("dp", "expert")),
        P(("dp", "expert")),
        P(("dp", "expert")),
        P(None, "expert", None, "dp"),
        P(None, "expert", "dp", None),
        P(("dp", "expert"), None),
    )
    return jax.shard_map(
        per_device,
        mesh=mesh,
        in_specs=placed,
        out_specs=(
            P(("dp", "expert"), None),
            P(("dp", "expert"), None),
            P(("dp", "expert")),
            P(("dp", "expert")),
            P(("dp", "expert")),
            P(("dp", "expert")),
            P(("dp", "expert")),
            P(None, "expert", None, "dp"),
            P(None, "expert", "dp", None),
        ),
        check_vma=False,
    )
```

profile of v0, /device:TPU:0, one launch (start us, length us, event | category | flops | bytes accessed | tf_op | source)
XLA Modules:
  0.0 1450.3 jit_solution(11554806207610799820)
XLA Ops:
  20.4 42.2 %all-reduce.9 = (bf16[3072]{0:T(1024)(128)(2,1)S(1)}, bf16[768]{0:T(1024)(128)(2,1)S(1)}) all-reduce(bf16[3072]{0:T(1024)(128)(2,1)S(1)} %dynamic-update-slice, bf16[768]{0:T(1024)(128)(2,1)S(1)} %dynamic-update-slice.1), channel_id=1, replica_groups=mesh['dp'=4,'expert'=8] {'dp','expert'}, use_global_device_ids=true, to_apply=%add | all-reduce | flops 3840 | bytes 15360
  69.2 41.0 %all-gather.4 = bf16[32,1,384]{2,1,0:T(2,128)(2,1)S(1)} all-gather(bf16[1,1,384]{2,1,0:T(2,128)(2,1)S(1)} %reshape.1118), channel_id=1, replica_groups=mesh['dp'=4,'expert'=8] {'dp','expert'}, dimensions={0}, use_global_device_ids=true | all-gather | bytes 25344 | tf_op jit(solution)/shard_map/all_gather | solution.py:156
  135.8 10.1 all-gather.12.cloned.1.call-done
  206.7 10.1 all-to-all-done.4
  220.9 14.6 %all-gather.16.cloned.1.call-done = bf16[1,1,768,3072]{3,2,1,0:T(8,128)(2,1)} async-done(((bf16[1,1,768,768]{3,2,1,0:T(8,128)(2,1)}), bf16[1,1,768,3072]{3,2,1,0:T(8,128)(2,1)}) %all-gather.16.cloned.1.call-update) | async-done | bytes 4718608 | tf_op jit(solution)/shard_map/all_gather | solution.py:174
  243.5 81.3 %all-gather.18.cloned.1.call-done = bf16[1,1,3072,768]{3,2,1,0:T(8,128)(2,1)} async-done(((bf16[1,1,768,768]{3,2,1,0:T(8,128)(2,1)}), bf16[1,1,3072,768]{3,2,1,0:T(8,128)(2,1)}) %all-gather.18.cloned.1.call-update) | async-done | bytes 4718608 | tf_op jit(solution)/shard_map/all_gather | solution.py:175
  324.8 8.8 fusion.121
  360.1 8.8 all-to-all-done.1
  437.7 65.7 %all-gather.22.cloned.1.call-done = bf16[1,1,3072,768]{3,2,1,0:T(8,128)(2,1)} async-done(((bf16[1,1,768,768]{3,2,1,0:T(8,128)(2,1)}), bf16[1,1,3072,768]{3,2,1,0:T(8,128)(2,1)}) %all-gather.22.cloned.1.call-update) | async-done | bytes 4718608 | tf_op jit(solution)/shard_map/all_gather | solution.py:175
  503.4 9.8 fusion.33
  517.4 8.8 fusion.133
  538.7 9.9 fusion.19
  558.7 8.8 fusion.130
  671.9 8.7 fusion.12
  690.3 8.7 fusion.26
  710.4 11.1 all-to-all-done.15
  765.9 11.7 pad_maximum_fusion
  777.7 15.3 %copy.268 = f32[2,3,768,768]{3,2,1,0:T(8,128)} copy(f32[2,3,768,768]{2,3,1,0:T(8,128)} %pad_maximum_fusion) | data formatting | bytes 28311552 | tf_op jit(solution)/shard_map/stack | solution.py:387
  792.9 15.2 %reshape.1101 = f32[3538944]{0:T(1024)} reshape(f32[2,3,768,768]{3,2,1,0:T(8,128)} %copy.268) | data formatting | bytes 28311552 | tf_op jit(solution)/shard_map/reshape | solution.py:387
  814.3 9.2 fusion.69
  912.4 39.0 %all-reduce.7 = (f32[3072]{0:T(1024)S(1)}, f32[768]{0:T(1024)S(1)}, f32[12288]{0:T(1024)S(1)}) all-reduce(f32[3072]{0:T(1024)S(1)} %reshape.1103, f32[768]{0:T(1024)S(1)} %reshape.1104, f32[12288]{0:T(1024)S(1)} %reshape.1105), channel_id=8, replica_groups=mesh['dp'=4,'expert'=8] {'dp','expert'}, use_global_device_ids=true, to_apply=%region_70.71.clone | all-reduce | flops 16128 | bytes 129024
  956.1 155.0 %all-reduce.12.cloned.1.call-done = (f32[3538944]{0:T(1024)}, f32[1179648]{0:T(1024)}) async-done(((f32[3538944]{0:T(1024)}, f32[1179648]{0:T(1024)}), (f32[3538944]{0:T(1024)}, f32[1179648]{0:T(1024)})) %all-reduce.12.cloned.1.call-update) | async-done | bytes 18874384
  1114.5 160.3 %reduce-scatter.5.cloned.1.call-done = bf16[2,1,768,768]{3,2,1,0:T(8,128)(2,1)} async-done(((bf16[2,1,3072,768]{3,2,1,0:T(8,128)(2,1)}), bf16[2,1,768,768]{3,2,1,0:T(8,128)(2,1)}) %reduce-scatter.5.cloned.1.call-update) | async-done | bytes 2359312 | tf_op jit(solution)/shard_map/reduce_scatter | solution.py:406
  1279.0 160.3 %reduce-scatter.3.cloned.1.call-done = bf16[2,1,768,768]{3,2,1,0:T(8,128)(2,1)} async-done(((bf16[2,1,768,3072]{3,2,1,0:T(8,128)(2,1)}), bf16[2,1,768,768]{3,2,1,0:T(8,128)(2,1)}) %reduce-scatter.3.cloned.1.call-update) | async-done | bytes 2359312 | tf_op jit(solution)/shard_map/reduce_scatter | solution.py:403
  (877 shorter events, 518.2 us)
Async XLA Ops:
  7.2 121.7 %all-gather.14.cloned.1.call-start = ((), (), s32[]{:S(2)}) async-start(), calls=%async_computation.19 | async-start | bytes 2433024 | tf_op jit(solution)/shard_map/all_gather | solution.py:153
  7.9 138.0 %all-gather.12.cloned.1.call-start = ((), (), s32[]{:S(2)}) async-start(), calls=%async_computation.18 | async-start | bytes 7299072 | tf_op jit(solution)/shard_map/all_gather | solution.py:152
  8.7 226.8 %all-gather.16.cloned.1.call-start = ((), (), s32[]{:S(2)}) async-start(), calls=%async_computation.22 | async-start | bytes 5898240 | tf_op jit(solution)/shard_map/all_gather | solution.py:174
  11.9 312.9 %all-gather.18.cloned.1.call-start = ((), (), s32[]{:S(2)}) async-start(), calls=%async_computation.23 | async-start | bytes 5898240 | tf_op jit(solution)/shard_map/all_gather | solution.py:175
  15.2 406.3 %all-gather.20.cloned.1.call-start = ((), (), s32[]{:S(2)}) async-start(), calls=%async_computation.24 | async-start | bytes 5898240 | tf_op jit(solution)/shard_map/all_gather | solution.py:174
  15.8 487.5 %all-gather.22.cloned.1.call-start = ((), (), s32[]{:S(2)}) async-start(), calls=%async_computation.25 | async-start | bytes 5898240 | tf_op jit(solution)/shard_map/all_gather | solution.py:175
  199.9 16.8 %all-to-all-start.4 = ((bf16[8,64,768]{2,1,0:T(8,128)(2,1)}), bf16[8,64,768]{2,1,0:T(8,128)(2,1)}, u32[]{:S(2)}, u32[]{:S(2)}) async-start(bf16[8,64,768]{2,1,0:T(8,128)(2,1)} %convolution_convert_fusion.9), calls=%async_computation.4 | async-start | bytes 1572864 | tf_op jit(solution)/shard_map/all_to_all | solution.py:206
  216.8 116.7 %all-to-all-start = ((bf16[8,64,768]{2,1,0:T(8,128)(2,1)}), bf16[8,64,768]{2,1,0:T(8,128)(2,1)S(1)}, u32[]{:S(2)}, u32[]{:S(2)}) async-start(bf16[8,64,768]{2,1,0:T(8,128)(2,1)} %convolution_convert_fusion.11), calls=%async_computation | async-start | bytes 1572864 | tf_op jit(solution)/shard_map/all_to_all | solution.py:206
  333.5 18.3 %all-to-all-start.5 = ((bf16[8,64,768]{2,1,0:T(8,128)(2,1)}), bf16[8,64,768]{2,1,0:T(8,128)(2,1)}, u32[]{:S(2)}, u32[]{:S(2)}) async-start(bf16[8,64,768]{2,1,0:T(8,128)(2,1)} %bitcast.482), calls=%async_computation.5 | async-start | bytes 1572864 | tf_op jit(solution)/shard_map/all_to_all | solution.py:215
  351.9 17.0 %all-to-all-start.1 = ((bf16[8,64,768]{2,1,0:T(8,128)(2,1)}), bf16[8,64,768]{2,1,0:T(8,128)(2,1)}, u32[]{:S(2)}, u32[]{:S(2)}) async-start(bf16[8,64,768]{2,1,0:T(8,128)(2,1)} %bitcast.479), calls=%async_computation.1 | async-start | bytes 1572864 | tf_op jit(solution)/shard_map/all_to_all | solution.py:215
  399.6 16.8 %all-to-all-start.6 = ((bf16[8,64,768]{2,1,0:T(8,128)(2,1)}), bf16[8,64,768]{2,1,0:T(8,128)(2,1)}, u32[]{:S(2)}, u32[]{:S(2)}) async-start(bf16[8,64,768]{2,1,0:T(8,128)(2,1)} %convolution_convert_fusion.8), calls=%async_computation.6 | async-start | bytes 1572864 | tf_op jit(solution)/shard_map/all_to_all | solution.py:206
  416.4 17.0 %all-to-all-start.12 = ((bf16[8,64,768]{2,1,0:T(8,128)(2,1)}), bf16[8,64,768]{2,1,0:T(8,128)(2,1)}, u32[]{:S(2)}, u32[]{:S(2)}) async-start(bf16[8,64,768]{2,1,0:T(8,128)(2,1)} %convolution_convert_fusion.5), calls=%async_computation.12 | async-start | bytes 1572864 | tf_op jit(solution)/shard_map/all_to_all | solution.py:320
  433.4 79.8 %all-to-all-start.2 = ((bf16[8,64,768]{2,1,0:T(8,128)(2,1)}), bf16[8,64,768]{2,1,0:T(8,128)(2,1)}, u32[]{:S(2)}, u32[]{:S(2)}) async-start(bf16[8,64,768]{2,1,0:T(8,128)(2,1)} %convolution_convert_fusion.10), calls=%async_computation.2 | async-start | bytes 1572864 | tf_op jit(solution)/shard_map/all_to_all | solution.py:206
  513.2 20.8 %all-to-all-start.8 = ((bf16[8,64,768]{2,1,0:T(8,128)(2,1)}), bf16[8,64,768]{2,1,0:T(8,128)(2,1)}, u32[]{:S(2)}, u32[]{:S(2)}) async-start(bf16[8,64,768]{2,1,0:T(8,128)(2,1)} %convolution_convert_fusion.7), calls=%async_computation.8 | async-start | bytes 1572864 | tf_op jit(solution)/shard_map/all_to_all | solution.py:320
  534.0 20.4 %all-to-all-start.7 = ((bf16[8,64,768]{2,1,0:T(8,128)(2,1)}), bf16[8,64,768]{2,1,0:T(8,128)(2,1)}, u32[]{:S(2)}, u32[]{:S(2)}) async-start(bf16[8,64,768]{2,1,0:T(8,128)(2,1)} %bitcast.481), calls=%async_computation.7 | async-start | bytes 1572864 | tf_op jit(solution)/shard_map/all_to_all | solution.py:215
  554.4 16.9 %all-to-all-start.13 = ((bf16[8,64,768]{2,1,0:T(8,128)(2,1)}), bf16[8,64,768]{2,1,0:T(8,128)(2,1)}, u32[]{:S(2)}, u32[]{:S(2)}) async-start(bf16[8,64,768]{2,1,0:T(8,128)(2,1)} %bitcast.483), calls=%async_computation.13 | async-start | bytes 1572864 | tf_op jit(solution)/shard_map/all_to_all | solution.py:341
  588.1 16.8 %all-to-all-start.9 = ((bf16[8,64,768]{2,1,0:T(8,128)(2,1)}), bf16[8,64,768]{2,1,0:T(8,128)(2,1)}, u32[]{:S(2)}, u32[]{:S(2)}) async-start(bf16[8,64,768]{2,1,0:T(8,128)(2,1)} %bitcast.478), calls=%async_computation.9 | async-start | bytes 1572864 | tf_op jit(solution)/shard_map/all_to_all | solution.py:341
  651.4 16.8 %all-to-all-start.10 = ((bf16[8,64,768]{2,1,0:T(8,128)(2,1)}), bf16[8,64,768]{2,1,0:T(8,128)(2,1)}, u32[]{:S(2)}, u32[]{:S(2)}) async-start(bf16[8,64,768]{2,1,0:T(8,128)(2,1)} %convolution_convert_fusion.6), calls=%async_computation.10 | async-start | bytes 1572864 | tf_op jit(solution)/shard_map/all_to_all | solution.py:320
  668.2 17.7 %all-to-all-start.14 = ((bf16[8,64,768]{2,1,0:T(8,128)(2,1)}), bf16[8,64,768]{2,1,0:T(8,128)(2,1)S(1)}, u32[]{:S(2)}, u32[]{:S(2)}) async-start(bf16[8,64,768]{2,1,0:T(8,128)(2,1)} %convolution_convert_fusion.4), calls=%async_computation.14 | async-start | bytes 1572864 | tf_op jit(solution)/shard_map/all_to_all | solution.py:320
  685.9 18.5 %all-to-all-start.11 = ((bf16[8,64,768]{2,1,0:T(8,128)(2,1)}), bf16[8,64,768]{2,1,0:T(8,128)(2,1)S(1)}, u32[]{:S(2)}, u32[]{:S(2)}) async-start(bf16[8,64,768]{2,1,0:T(8,128)(2,1)} %bitcast.84), calls=%async_computation.11 | async-start | bytes 1572864 | tf_op jit(solution)/shard_map/all_to_all | solution.py:341
  704.4 17.1 %all-to-all-start.15 = ((bf16[8,64,768]{2,1,0:T(8,128)(2,1)}), bf16[8,64,768]{2,1,0:T(8,128)(2,1)}, u32[]{:S(2)}, u32[]{:S(2)}) async-start(bf16[8,64,768]{2,1,0:T(8,128)(2,1)} %bitcast.108), calls=%async_computation.15 | async-start | bytes 1572864 | tf_op jit(solution)/shard_map/all_to_all | solution.py:341
  708.8 402.4 %all-reduce.12.cloned.1.call-start = ((), (), s32[]{:S(2)}) async-start(), calls=%async_computation.26 | async-start | bytes 37748736
  808.2 466.6 %reduce-scatter.5.cloned.1.call-start = ((), (), s32[]{:S(2)}) async-start(), calls=%async_computation.21 | async-start | bytes 11796480 | tf_op jit(solution)/shard_map/reduce_scatter | solution.py:406
  846.3 593.0 %reduce-scatter.3.cloned.1.call-start = ((), (), s32[]{:S(2)}) async-start(), calls=%async_computation.20 | async-start | bytes 11796480 | tf_op jit(solution)/shard_map/reduce_scatter | solution.py:403
  (273 other events, 3235.2 us)
Sparse Core Ops, SparseCore 0:
  10.9 60.5 all-gather.13
  74.4 71.4 all-gather.11
  147.5 87.9 all-gather.15
  236.9 87.8 all-gather.17
  326.2 87.8 all-gather.19
  415.5 87.8 all-gather.21
  808.3 302.7 all-reduce.11
  1113.5 161.2 reduce-scatter.4
  1277.2 162.1 reduce-scatter.2
where the time goes:
time: 1460 us; the launch traced here: 1450 us
  waiting for transfers between devices  699 us (48%)
  matrix products  311 us (21%)
  local copies, waits for them, and re-layouts  166 us (11%)
  blocking collectives  122 us (8%)
  starting transfers between devices  68.4 us (5%)
  other arithmetic  66.5 us (5%)
  between operations  17.6 us (1%)
    reduce_scatter x1, waiting for transfers between devices, per_device(): lax.psum_scatter(jnp.stack(acc_ein)[:, None].astype(jnp.bfloat16), 'dp',...  160 us
    reduce_scatter x1, waiting for transfers between devices, per_device(): lax.psum_scatter(jnp.stack(acc_eout)[:, None].astype(jnp.bfloat16), 'dp',...  160 us
    unnamed x10, waiting for transfers between devices  158 us
    all_gather x2, waiting for transfers between devices, per_device(): lax.all_gather(expert_out[layer_no], 'dp', axis=1, tiled=True)  147 us
    unnamed x2, blocking collectives  81.3 us
    all_gather x1, blocking collectives, per_device(): lax.all_gather(router, ('dp', 'expert'), axis=0, tiled=True)  41 us
    dot_general x4, matrix products, per_device(): jnp.einsum('rd,fd->rf', flat_grad, weight_out, preferred_element_type=jnp...  37.2 us
    dot_general x4, matrix products, per_device(): jnp.dot(expert_hidden, weight_out, preferred_element_type=jnp.float32)  33.3 us
  transfers between devices with their start and end apart: 25, of which 16 were waited for; matrix products, arithmetic and copies ran while one was open for 27% of the time, Pallas kernels for 0%

commit v1 on v0

--- a/solution.py
+++ b/solution.py
@@ -123,11 +123,43 @@
         .reshape(3, row_count, -1)
         .astype(jnp.bfloat16)
     )
-    grad_qkv = jnp.einsum("td,kte->kde", normed, grad_proj, preferred_element_type=jnp.float32)
     grad_normed = jnp.einsum(
         "kte,kde->td", grad_proj, weights_qkv, preferred_element_type=jnp.float32
     )
-    return (grad_qkv, grad_table, grad_normed)
+    return (grad_proj, grad_table, grad_normed)
+
+
+def lane_rows(flat):
+    return flat.reshape(flat.shape[0] // 128, 128)
+
+
+def pack_small(parts, lead):
+    joined = jnp.concatenate([part.reshape(lead, -1) for part in parts], axis=1)
+    room = -(-joined.shape[1] // 2048) * 2048
+    joined = jnp.pad(joined, ((0, 0), (0, room - joined.shape[1])))
+    return joined.reshape(lead, room // 128, 128)
+
+
+def unpack_small(block, sizes):
+    flat = block.reshape(block.shape[0], -1)
+    pieces = []
+    start = 0
+    for size in sizes:
+        pieces.append(flat[:, start : start + size])
+        start += size
+    return pieces
+
+
+def dense_sums(grad_qkv, grad_out, dp_count, expert_lanes):
+    joined = jnp.concatenate(
+        [
+            grad_qkv.astype(jnp.bfloat16).reshape(dp_count * expert_lanes, -1, 128),
+            grad_out.astype(jnp.bfloat16).reshape(dp_count * expert_lanes, -1, 128),
+        ],
+        axis=1,
+    ).reshape(dp_count, expert_lanes, -1, 128)
+    swapped = lax.all_to_all(joined, "expert", split_axis=1, concat_axis=1, tiled=True)
+    return jnp.sum(swapped.astype(jnp.float32), axis=1)
 
 
 def per_device(
@@ -148,20 +180,49 @@
     layer_count = LAYERS
     model_width = tokens.shape[1]
     expert_count = expert_in.shape[1] * lax.axis_size("expert")
-    full_qkv, full_out, full_gain, full_table, full_router = (
-        lax.all_gather(qkv_weights, ("dp", "expert"), axis=0, tiled=True),
-        lax.all_gather(out_weights, ("dp", "expert"), axis=0, tiled=True),
-        lax.all_gather(gains, ("dp", "expert"), axis=0, tiled=True),
-        lax.all_gather(bias_table, ("dp", "expert"), axis=0, tiled=True),
-        lax.all_gather(router, ("dp", "expert"), axis=0, tiled=True),
-    )
-    full_qkv = full_qkv.reshape(layer_count, 3, model_width, model_width)
-    full_out = full_out.reshape(layer_count, model_width, model_width)
+    dp_count = lax.axis_size("dp")
+    expert_lanes = lax.axis_size("expert")
+    device_count = dp_count * expert_lanes
+    small_sizes = (gains.shape[0], bias_table.shape[0], router.shape[0])
+    qkv_rows = qkv_weights.shape[0] // 128
+    out_rows = out_weights.shape[0] // 128
+    own_pack = jnp.concatenate(
+        [
+            lane_rows(qkv_weights),
+            lane_rows(out_weights),
+            pack_small((gains, bias_table, router), 1)[0],
+        ],
+        axis=0,
+    )
+    every_pack = lax.all_gather(own_pack, ("dp", "expert"), axis=0, tiled=False)
+    full_qkv = every_pack[:, :qkv_rows].reshape(layer_count, 3, model_width, model_width)
+    full_out = every_pack[:, qkv_rows : qkv_rows + out_rows].reshape(
+        layer_count, model_width, model_width
+    )
+    full_gain, full_table, full_router = unpack_small(
+        every_pack[:, qkv_rows + out_rows :], small_sizes
+    )
     full_gain = full_gain.reshape(layer_count, 2, model_width)
     full_router = full_router.reshape(layer_count, model_width, expert_count)
     bias_rows = full_table.reshape(layer_count, NB, H)
     capacity = 2 * block_rows // expert_count
     bucket_onehot = bucket_table(block_rows, NB)
+    weights = [
+        (
+            lax.all_gather(expert_in[layer_no], "dp", axis=2, tiled=True)[0],
+            lax.all_gather(expert_out[layer_no], "dp", axis=1, tiled=True)[0],
+        )
+        for layer_no in range(layer_count)
+    ]
+    rel_biases = [
+        jnp.einsum(
+            "ijb,bh->hij",
+            bucket_onehot,
+            bias_rows[layer_no],
+            preferred_element_type=jnp.float32,
+        )
+        for layer_no in range(layer_count)
+    ]
     saved = []
     mixed_parts = []
     for batch_no in range(micro_count):
@@ -170,19 +231,9 @@
         allowed = same_sequence(lengths[batch_no], block_rows)
         batch_saved = []
         for layer_no in range(layer_count):
-            layer_in, layer_out = (
-                lax.all_gather(expert_in[layer_no], "dp", axis=2, tiled=True),
-                lax.all_gather(expert_out[layer_no], "dp", axis=1, tiled=True),
-            )
-            weight_in = layer_in[0]
-            weight_out = layer_out[0]
+            weight_in, weight_out = weights[layer_no]
             gain_pair = full_gain[layer_no].astype(jnp.float32)
-            rel_bias = jnp.einsum(
-                "ijb,bh->hij",
-                bucket_onehot,
-                bias_rows[layer_no],
-                preferred_element_type=jnp.float32,
-            )
+            rel_bias = rel_biases[layer_no]
             unit_one, recip_one = unit_scale(stream)
             normed = (unit_one * gain_pair[0]).astype(jnp.bfloat16)
             projected, attended, log_total = attend_forward(
@@ -249,37 +300,25 @@
         saved.append(batch_saved)
         mixed_parts.append(stream)
     mixed = jnp.concatenate(mixed_parts, axis=0).astype(jnp.bfloat16)
-    back_qkv, back_out, back_gain, back_table, back_router = (
-        lax.all_gather(qkv_weights, ("dp", "expert"), axis=0, tiled=True),
-        lax.all_gather(out_weights, ("dp", "expert"), axis=0, tiled=True),
-        lax.all_gather(gains, ("dp", "expert"), axis=0, tiled=True),
-        lax.all_gather(bias_table, ("dp", "expert"), axis=0, tiled=True),
-        lax.all_gather(router, ("dp", "expert"), axis=0, tiled=True),
-    )
-    back_qkv = back_qkv.reshape(layer_count, 3, model_width, model_width)
-    back_out = back_out.reshape(layer_count, model_width, model_width)
-    back_gain = back_gain.reshape(layer_count, 2, model_width)
-    back_router = back_router.reshape(layer_count, model_width, expert_count)
-    back_rows = back_table.reshape(layer_count, NB, H)
-    acc_qkv = [
-        jnp.zeros((3, model_width, model_width), jnp.float32) for layer_no in range(layer_count)
-    ]
-    acc_out = [
-        jnp.zeros((model_width, model_width), jnp.float32) for layer_no in range(layer_count)
-    ]
     acc_gain = [jnp.zeros((2, model_width), jnp.float32) for layer_no in range(layer_count)]
     acc_table = [jnp.zeros((NB, H), jnp.float32) for layer_no in range(layer_count)]
     acc_router = [
         jnp.zeros((model_width, expert_count), jnp.float32) for layer_no in range(layer_count)
     ]
-    acc_ein = [jnp.zeros((model_width, FF), jnp.float32) for layer_no in range(layer_count)]
-    acc_eout = [jnp.zeros((FF, model_width), jnp.float32) for layer_no in range(layer_count)]
-    grad_parts = []
-    for batch_no in range(micro_count):
-        row_start = batch_no * block_rows
-        allowed = same_sequence(lengths[batch_no], block_rows)
-        grad_stream = cotangent[row_start : row_start + block_rows].astype(jnp.float32)
-        for layer_no in reversed(range(layer_count)):
+    grad_streams = [
+        cotangent[batch_no * block_rows : (batch_no + 1) * block_rows].astype(jnp.float32)
+        for batch_no in range(micro_count)
+    ]
+    allowed_parts = [same_sequence(lengths[batch_no], block_rows) for batch_no in range(micro_count)]
+    ein_parts = [None] * layer_count
+    eout_parts = [None] * layer_count
+    dense_parts = [None] * layer_count
+    for layer_no in reversed(range(layer_count)):
+        kept_hidden, kept_flat_grad, kept_rows, kept_inner = ([], [], [], [])
+        kept_attended, kept_branch, kept_normed, kept_proj = ([], [], [], [])
+        for batch_no in range(micro_count):
+            grad_stream = grad_streams[batch_no]
+            allowed = allowed_parts[batch_no]
             (
                 stream,
                 after_attn,
@@ -296,13 +335,8 @@
                 arrived,
                 inner_act,
             ) = saved[batch_no][layer_no]
-            layer_in, layer_out = (
-                lax.all_gather(expert_in[layer_no], "dp", axis=2, tiled=True),
-                lax.all_gather(expert_out[layer_no], "dp", axis=1, tiled=True),
-            )
-            weight_in = layer_in[0]
-            weight_out = layer_out[0]
-            gain_pair = back_gain[layer_no].astype(jnp.float32)
+            weight_in, weight_out = weights[layer_no]
+            gain_pair = full_gain[layer_no].astype(jnp.float32)
             grad_mix = (gate_value[:, None] * grad_stream).astype(jnp.bfloat16)
             grad_gate = jnp.sum(grad_stream * expert_mix, axis=1)
             grad_logits = (
@@ -312,7 +346,7 @@
                 "td,te->de", normed_two, grad_logits, preferred_element_type=jnp.float32
             )
             grad_normed_two = jnp.einsum(
-                "te,de->td", grad_logits, back_router[layer_no], preferred_element_type=jnp.float32
+                "te,de->td", grad_logits, full_router[layer_no], preferred_element_type=jnp.float32
             )
             grad_slots = jnp.einsum(
                 "tec,td->ecd", slot_table, grad_mix, preferred_element_type=jnp.float32
@@ -324,17 +358,15 @@
             flat_rows = arrived.reshape(-1, model_width)
             flat_inner = inner_act.reshape(flat_grad.shape[0], -1)
             hidden = jax.nn.gelu(flat_inner).astype(jnp.bfloat16)
-            acc_eout[layer_no] = acc_eout[layer_no] + jnp.einsum(
-                "rf,rd->fd", hidden, flat_grad, preferred_element_type=jnp.float32
-            )
+            kept_hidden.append(hidden)
+            kept_flat_grad.append(flat_grad)
             grad_hidden = jnp.einsum(
                 "rd,fd->rf", flat_grad, weight_out, preferred_element_type=jnp.float32
             )
             unused, pull_back = jax.vjp(jax.nn.gelu, flat_inner)
             grad_inner = pull_back(grad_hidden)[0].astype(jnp.bfloat16)
-            acc_ein[layer_no] = acc_ein[layer_no] + jnp.einsum(
-                "rd,rf->df", flat_rows, grad_inner, preferred_element_type=jnp.float32
-            )
+            kept_rows.append(flat_rows)
+            kept_inner.append(grad_inner)
             grad_rows = jnp.einsum(
                 "rf,df->rd", grad_inner, weight_in, preferred_element_type=jnp.float32
             ).astype(jnp.bfloat16)
@@ -352,71 +384,92 @@
             grad_after, gain_two = norm_back(grad_normed_two, unit_two, recip_two, gain_pair[1])
             grad_after = grad_stream + grad_after
             grad_branch = grad_after.astype(jnp.bfloat16)
-            acc_out[layer_no] = acc_out[layer_no] + jnp.einsum(
-                "td,te->de", attended, grad_branch, preferred_element_type=jnp.float32
-            )
+            kept_attended.append(attended)
+            kept_branch.append(grad_branch)
             grad_attended = jnp.einsum(
-                "te,de->td", grad_branch, back_out[layer_no], preferred_element_type=jnp.float32
+                "te,de->td", grad_branch, full_out[layer_no], preferred_element_type=jnp.float32
             ).astype(jnp.bfloat16)
-            rel_bias = jnp.einsum(
-                "ijb,bh->hij",
-                bucket_onehot,
-                back_rows[layer_no],
-                preferred_element_type=jnp.float32,
-            )
-            grad_qkv, grad_table, grad_normed = attend_backward(
+            rel_bias = rel_biases[layer_no]
+            grad_proj, grad_table, grad_normed = attend_backward(
                 grad_attended,
                 normed,
                 projected,
                 rel_bias,
                 allowed,
                 log_total,
-                back_qkv[layer_no],
+                full_qkv[layer_no],
                 bucket_onehot,
             )
-            acc_qkv[layer_no] = acc_qkv[layer_no] + grad_qkv
+            kept_normed.append(normed)
+            kept_proj.append(grad_proj)
             acc_table[layer_no] = acc_table[layer_no] + grad_table
             unit_one, recip_one = unit_scale(stream)
             grad_input, gain_one = norm_back(grad_normed, unit_one, recip_one, gain_pair[0])
             acc_gain[layer_no] = acc_gain[layer_no] + jnp.stack([gain_one, gain_two])
-            grad_stream = grad_after + grad_input
-        grad_parts.append(grad_stream)
-    input_grad = jnp.concatenate(grad_parts, axis=0)
-    param_sums = (
-        lax.psum_scatter(
-            jnp.stack(acc_qkv).reshape(-1), ("dp", "expert"), scatter_dimension=0, tiled=True
+            grad_streams[batch_no] = grad_after + grad_input
+        eout_full = jnp.einsum(
+            "rf,rd->fd",
+            jnp.concatenate(kept_hidden, axis=0),
+            jnp.concatenate(kept_flat_grad, axis=0),
+            preferred_element_type=jnp.float32,
+        ).astype(jnp.bfloat16)
+        eout_parts[layer_no] = lax.psum_scatter(eout_full, "dp", scatter_dimension=0, tiled=True)
+        ein_full = jnp.einsum(
+            "rf,rd->fd",
+            jnp.concatenate(kept_inner, axis=0),
+            jnp.concatenate(kept_rows, axis=0),
+            preferred_element_type=jnp.float32,
+        ).astype(jnp.bfloat16)
+        ein_parts[layer_no] = lax.psum_scatter(ein_full, "dp", scatter_dimension=0, tiled=True)
+        grad_out = jnp.einsum(
+            "td,te->de",
+            jnp.concatenate(kept_attended, axis=0),
+            jnp.concatenate(kept_branch, axis=0),
+            preferred_element_type=jnp.float32,
+        )
+        grad_qkv = jnp.einsum(
+            "td,kte->kde",
+            jnp.concatenate(kept_normed, axis=0),
+            jnp.concatenate(kept_proj, axis=1),
+            preferred_element_type=jnp.float32,
+        )
+        dense_parts[layer_no] = dense_sums(
+            grad_qkv, grad_out, dp_count // layer_count, expert_lanes
+        )
+    input_grad = jnp.concatenate(grad_streams, axis=0)
+    small_pack = pack_small(
+        (jnp.stack(acc_gain), jnp.stack(acc_table), jnp.stack(acc_router)), device_count
+    )
+    small_sum = jnp.sum(
+        lax.all_to_all(
+            small_pack.astype(jnp.bfloat16).reshape(dp_count, expert_lanes, -1, 128),
+            "expert",
+            split_axis=1,
+            concat_axis=1,
+            tiled=True,
+        ).astype(jnp.float32),
+        axis=1,
+    )
+    dense_pack = jnp.concatenate(
+        [jnp.concatenate(dense_parts, axis=0), small_sum], axis=1
+    ).astype(jnp.bfloat16)
+    own_sum = jnp.sum(
+        lax.all_to_all(dense_pack, "dp", split_axis=0, concat_axis=0, tiled=True).astype(
+            jnp.float32
         ),
-        lax.psum_scatter(
-            jnp.stack(acc_out).reshape(-1), ("dp", "expert"), scatter_dimension=0, tiled=True
-        ),
-        lax.psum_scatter(
-            jnp.stack(acc_gain).reshape(-1), ("dp", "expert"), scatter_dimension=0, tiled=True
-        ),
-        lax.psum_scatter(
-            jnp.stack(acc_table).reshape(-1), ("dp", "expert"), scatter_dimension=0, tiled=True
-        ),
-        lax.psum_scatter(
-            jnp.stack(acc_router).reshape(-1), ("dp", "expert"), scatter_dimension=0, tiled=True
-        ),
-    )
-    expert_sums = (
-        lax.psum_scatter(
-            jnp.stack(acc_ein)[:, None].astype(jnp.bfloat16), "dp", scatter_dimension=3, tiled=True
-        ).astype(jnp.float32),
-        lax.psum_scatter(
-            jnp.stack(acc_eout)[:, None].astype(jnp.bfloat16), "dp", scatter_dimension=2, tiled=True
-        ).astype(jnp.float32),
-    )
+        axis=0,
+    )
+    own_small = unpack_small(own_sum[None, qkv_rows + out_rows :], small_sizes)
     return (
         mixed,
         input_grad,
-        param_sums[0],
-        param_sums[1],
-        param_sums[2],
-        param_sums[3],
-        param_sums[4],
-        expert_sums[0],
-        expert_sums[1],
+        own_sum[:qkv_rows].reshape(-1),
+        own_sum[qkv_rows : qkv_rows + out_rows].reshape(-1),
+        own_small[0][0],
+        own_small[1][0],
+        own_small[2][0],
+        jnp.stack([jnp.transpose(part) for part in ein_parts]).astype(jnp.float32)[:, None],
+        jnp.stack(eout_parts).astype(jnp.float32)[:, None],
     )
 
 

time: 1460 us -> 1030 us (0.71)
  waiting for transfers between devices: 699 us -> 396 us
  blocking collectives: 122 us -> 0 us
  matrix products: 311 us -> 293 us
  starting transfers between devices: 68.4 us -> 84 us
    reduce_scatter x2 -> x4, waiting for transfers between devices: 321 us -> 0.01 us  [the longest x2 0.01 us: per_device(): lax.psum_scatter(ein_full, 'dp', scatter_dimension=0, tiled=True)]
    unnamed x10 -> x9, waiting for transfers between devices: 158 us -> 1.17 us
    all_to_all x0 -> x4, waiting for transfers between devices: none -> 125 us  [the longest x2 75.9 us: dense_sums(): lax.all_to_all(joined, 'expert', split_axis=1, concat_axis=1, tiled=True)]
    unnamed x2 -> x0, blocking collectives: 81.3 us -> none
    all_gather x6 -> x5, waiting for transfers between devices: 172 us -> 219 us  [the longest x2 139 us: per_device(): lax.all_gather(expert_out[layer_no], 'dp', axis=1, tiled=True)[0]]
    all_gather x1 -> x0, blocking collectives: 41 us -> none  [per_device(): lax.all_gather(router, ('dp', 'expert'), axis=0, tiled=True)]
    another operation x17 -> x15, other arithmetic: 33.7 us -> 4.09 us  [the longest x1 11.7 us: per_device(): jnp.stack(acc_qkv).reshape(-1)]
    dot_general x24 -> x16, matrix products: 84 us -> 60.1 us  [the longest x2 18.5 us: per_device(): jnp.einsum('rf,rd->fd', jnp.concatenate(kept_hidden, axis=0), jnp.concate...]
  transfers between devices with their start and end apart: 25 -> 29, of which waited for: 16 -> 19; matrix products, arithmetic and copies ran while one was open for 27% -> 48% of each run, Pallas kernels for 0% -> 0%
where the time goes in v1:
time: 1030 us; the launch traced here: 1020 us
  waiting for transfers between devices  396 us (38%)
  matrix products  293 us (28%)
  local copies, waits for them, and re-layouts  160 us (16%)
  starting transfers between devices  84 us (8%)
  other arithmetic  63.5 us (6%)
  between operations  18.1 us (2%)
    all_gather x2, waiting for transfers between devices, per_device(): lax.all_gather(expert_out[layer_no], 'dp', axis=1, tiled=True)[0]  139 us
    all_to_all x2, waiting for transfers between devices, dense_sums(): lax.all_to_all(joined, 'expert', split_axis=1, concat_axis=1, tiled=True)  75.9 us
    all_gather x1, waiting for transfers between devices, per_device(): every_pack = lax.all_gather(own_pack, ('dp', 'expert'), axis=0, tiled=False)  68.6 us
    all_to_all x1, waiting for transfers between devices, per_device(): lax.all_to_all(dense_pack, 'dp', split_axis=0, concat_axis=0, tiled=True)  48 us
    dot_general x4, matrix products, per_device(): jnp.einsum('rd,fd->rf', flat_grad, weight_out, preferred_element_type=jnp...  37.6 us
    dot_general x4, matrix products, per_device(): jnp.dot(expert_flat_rows, weight_in, preferred_element_type=jnp.float32)  36.8 us
    all_to_all x4, waiting for transfers between devices, per_device(): lax.all_to_all(grad_rows.reshape(arrived_grad.shape), 'expert', split_axi...  26.6 us
    dot_general x4, matrix products, per_device(): jnp.einsum('rf,df->rd', grad_inner, weight_in, preferred_element_type=jnp...  26.5 us
  transfers between devices with their start and end apart: 29, of which 19 were waited for; matrix products, arithmetic and copies ran while one was open for 48% of the time, Pallas kernels for 0%

profile of v1, /device:TPU:0, one launch (start us, length us, event | category | flops | bytes accessed | tf_op | source)
XLA Modules:
  0.0 1015.1 jit_solution(1618382524472274824)
XLA Ops:
  28.0 68.6 %all-gather.11.cloned.1.call-done = bf16[37376,128]{1,0:T(8,128)(2,1)} async-done(((bf16[1168,128]{1,0:T(8,128)(2,1)}), bf16[37376,128]{1,0:T(8,128)(2,1)}) %all-gather.11.cloned.1.call-update) | async-done | bytes 9568272 | tf_op jit(solution)/shard_map/all_gather | solution.py:197
  120.2 7.3 squeeze.73
  186.2 8.5 multiply_convert_fusion.1
  194.7 80.9 %all-gather.15.cloned.1.call-done = bf16[1,1,3072,768]{3,2,1,0:T(8,128)(2,1)} async-done(((bf16[1,1,768,768]{3,2,1,0:T(8,128)(2,1)}), bf16[1,1,3072,768]{3,2,1,0:T(8,128)(2,1)}) %all-gather.15.cloned.1.call-update) | async-done | bytes 4718608 | tf_op jit(solution)/shard_map/all_gather | solution.py:213
  286.3 8.0 multiply_convert_fusion.3
  307.7 11.2 %all-to-all-done.1 = bf16[8,64,768]{2,1,0:T(8,128)(2,1)} async-done(((bf16[8,64,768]{2,1,0:T(8,128)(2,1)}), bf16[8,64,768]{2,1,0:T(8,128)(2,1)}, u32[]{:S(2)}, u32[]{:S(2)}) %all-to-all-start.1) | async-done | bytes 786464 | tf_op jit(solution)/shard_map/all_to_all | solution.py:266
  355.7 9.3 all-gather.17.cloned.1.call-done
  365.0 10.3 %multiply_convert_fusion = (bf16[512,3072]{1,0:T(8,128)(2,1)}, f32[512,3072]{1,0:T(8,128)}) fusion(bf16[512,768]{1,0:T(8,128)(2,1)} %bitcast.72, bf16[1,1,768,3072]{3,2,1,0:T(8,128)(2,1)} %all-gather.17.cloned.1.call-done), kind=kOutput, calls=%fused_computation.59 | convolution fusion | flops 2430074880 | bytes 14942208 | tf_op jit(solution)/shard_map/dot_general | solution.py:261
  379.5 10.1 multiply_convert_fusion.2
  396.3 58.0 %all-gather.19.cloned.1.call-done = bf16[1,1,3072,768]{3,2,1,0:T(8,128)(2,1)} async-done(((bf16[1,1,768,768]{3,2,1,0:T(8,128)(2,1)}), bf16[1,1,3072,768]{3,2,1,0:T(8,128)(2,1)}) %all-gather.19.cloned.1.call-update) | async-done | bytes 4718608 | tf_op jit(solution)/shard_map/all_gather | solution.py:213
  454.3 10.0 fusion.33
  472.0 8.9 fusion.19
  482.6 8.3 fusion.56
  519.1 6.9 fusion.185
  539.5 9.0 all-to-all-done.13
  617.5 9.8 fusion.12
  630.0 8.9 fusion.26
  640.7 7.0 fusion.59
  649.7 9.7 fusion.50
  725.9 11.0 %all-to-all-done.15 = bf16[8,64,768]{2,1,0:T(8,128)(2,1)} async-done(((bf16[8,64,768]{2,1,0:T(8,128)(2,1)}), bf16[8,64,768]{2,1,0:T(8,128)(2,1)}, u32[]{:S(2)}, u32[]{:S(2)}) %all-to-all-start.15) | async-done | bytes 786464 | tf_op jit(solution)/shard_map/all_to_all | solution.py:373
  834.7 34.2 %all-to-all-done.17 = bf16[2,8,1152,128]{3,2,0,1:T(8,128)(2,1)} async-done(((bf16[2,8,1152,128]{3,2,0,1:T(8,128)(2,1)}), bf16[2,8,1152,128]{3,2,0,1:T(8,128)(2,1)}, u32[]{:S(2)}, u32[]{:S(2)}) %all-to-all-start.17) | async-done | bytes 4718624 | tf_op jit(solution)/shard_map/all_to_all | solution.py:161
  873.6 8.9 fusion.53
  886.6 41.7 %all-to-all-done.16 = bf16[2,8,1152,128]{3,2,0,1:T(8,128)(2,1)} async-done(((bf16[2,8,1152,128]{3,2,0,1:T(8,128)(2,1)}), bf16[2,8,1152,128]{3,2,0,1:T(8,128)(2,1)}, u32[]{:S(2)}, u32[]{:S(2)}) %all-to-all-start.16) | async-done | bytes 4718624 | tf_op jit(solution)/shard_map/all_to_all | solution.py:161
  942.7 48.0 %all-to-all-done.19 = bf16[4,1168,128]{2,1,0:T(8,128)(2,1)S(1)} async-done(((bf16[4,1168,128]{2,1,0:T(8,128)(2,1)}), bf16[4,1168,128]{2,1,0:T(8,128)(2,1)S(1)}, u32[]{:S(2)}, u32[]{:S(2)}) %all-to-all-start.19) | async-done | bytes 1196064 | tf_op jit(solution)/shard_map/all_to_all | solution.py:457
  (955 shorter events, 502.7 us)
Async XLA Ops:
  7.2 89.4 %all-gather.11.cloned.1.call-start = ((), (), s32[]{:S(2)}) async-start(), calls=%async_computation.28 | async-start | bytes 9867264 | tf_op jit(solution)/shard_map/all_gather | solution.py:197
  10.4 175.8 %all-gather.13.cloned.1.call-start = ((), (), s32[]{:S(2)}) async-start(), calls=%async_computation.29 | async-start | bytes 5898240 | tf_op jit(solution)/shard_map/all_gather | solution.py:212
  13.9 261.7 %all-gather.15.cloned.1.call-start = ((), (), s32[]{:S(2)}) async-start(), calls=%async_computation.30 | async-start | bytes 5898240 | tf_op jit(solution)/shard_map/all_gather | solution.py:213
  15.5 349.4 %all-gather.17.cloned.1.call-start = ((), (), s32[]{:S(2)}) async-start(), calls=%async_computation.31 | async-start | bytes 5898240 | tf_op jit(solution)/shard_map/all_gather | solution.py:212
  16.1 438.1 %all-gather.19.cloned.1.call-start = ((), (), s32[]{:S(2)}) async-start(), calls=%async_computation.32 | async-start | bytes 5898240 | tf_op jit(solution)/shard_map/all_gather | solution.py:213
  180.8 101.6 %all-to-all-start = ((bf16[8,64,768]{2,1,0:T(8,128)(2,1)}), bf16[8,64,768]{2,1,0:T(8,128)(2,1)S(1)}, u32[]{:S(2)}, u32[]{:S(2)}) async-start(bf16[8,64,768]{2,1,0:T(8,128)(2,1)} %convolution_convert_fusion.13), calls=%async_computation | async-start | bytes 1572864 | tf_op jit(solution)/shard_map/all_to_all | solution.py:257
  282.4 19.5 %all-to-all-start.5 = ((bf16[8,64,768]{2,1,0:T(8,128)(2,1)}), bf16[8,64,768]{2,1,0:T(8,128)(2,1)S(1)}, u32[]{:S(2)}, u32[]{:S(2)}) async-start(bf16[8,64,768]{2,1,0:T(8,128)(2,1)} %bitcast.58), calls=%async_computation.5 | async-start | bytes 1572864 | tf_op jit(solution)/shard_map/all_to_all | solution.py:266
  301.9 16.9 %all-to-all-start.1 = ((bf16[8,64,768]{2,1,0:T(8,128)(2,1)}), bf16[8,64,768]{2,1,0:T(8,128)(2,1)}, u32[]{:S(2)}, u32[]{:S(2)}) async-start(bf16[8,64,768]{2,1,0:T(8,128)(2,1)} %bitcast.23), calls=%async_computation.1 | async-start | bytes 1572864 | tf_op jit(solution)/shard_map/all_to_all | solution.py:266
  351.0 24.2 %all-to-all-start.2 = ((bf16[8,64,768]{2,1,0:T(8,128)(2,1)}), bf16[8,64,768]{2,1,0:T(8,128)(2,1)}, u32[]{:S(2)}, u32[]{:S(2)}) async-start(bf16[8,64,768]{2,1,0:T(8,128)(2,1)} %convolution_convert_fusion.12), calls=%async_computation.2 | async-start | bytes 1572864 | tf_op jit(solution)/shard_map/all_to_all | solution.py:257
  375.2 16.8 %all-to-all-start.12 = ((bf16[8,64,768]{2,1,0:T(8,128)(2,1)}), bf16[8,64,768]{2,1,0:T(8,128)(2,1)}, u32[]{:S(2)}, u32[]{:S(2)}) async-start(bf16[8,64,768]{2,1,0:T(8,128)(2,1)} %convolution_convert_fusion.7), calls=%async_computation.12 | async-start | bytes 1572864 | tf_op jit(solution)/shard_map/all_to_all | solution.py:354
  392.1 75.7 %all-to-all-start.8 = ((bf16[8,64,768]{2,1,0:T(8,128)(2,1)}), bf16[8,64,768]{2,1,0:T(8,128)(2,1)}, u32[]{:S(2)}, u32[]{:S(2)}) async-start(bf16[8,64,768]{2,1,0:T(8,128)(2,1)} %convolution_convert_fusion.9), calls=%async_computation.8 | async-start | bytes 1572864 | tf_op jit(solution)/shard_map/all_to_all | solution.py:354
  467.7 30.1 %all-to-all-start.7 = ((bf16[8,64,768]{2,1,0:T(8,128)(2,1)}), bf16[8,64,768]{2,1,0:T(8,128)(2,1)}, u32[]{:S(2)}, u32[]{:S(2)}) async-start(bf16[8,64,768]{2,1,0:T(8,128)(2,1)} %bitcast.493), calls=%async_computation.7 | async-start | bytes 1572864 | tf_op jit(solution)/shard_map/all_to_all | solution.py:266
  472.0 522.2 %reduce-scatter.7.cloned.1.call-start = ((), (), s32[]{:S(2)}) async-start(), calls=%async_computation.25 | async-start | bytes 5898240 | tf_op jit(solution)/shard_map/reduce_scatter | solution.py:423
  497.8 16.8 %all-to-all-start.3 = ((bf16[8,64,768]{2,1,0:T(8,128)(2,1)}), bf16[8,64,768]{2,1,0:T(8,128)(2,1)}, u32[]{:S(2)}, u32[]{:S(2)}) async-start(bf16[8,64,768]{2,1,0:T(8,128)(2,1)} %bitcast.495), calls=%async_computation.3 | async-start | bytes 1572864 | tf_op jit(solution)/shard_map/all_to_all | solution.py:266
  514.6 17.0 %all-to-all-start.9 = ((bf16[8,64,768]{2,1,0:T(8,128)(2,1)}), bf16[8,64,768]{2,1,0:T(8,128)(2,1)}, u32[]{:S(2)}, u32[]{:S(2)}) async-start(bf16[8,64,768]{2,1,0:T(8,128)(2,1)} %bitcast.494), calls=%async_computation.9 | async-start | bytes 1572864 | tf_op jit(solution)/shard_map/all_to_all | solution.py:373
  531.7 16.8 %all-to-all-start.13 = ((bf16[8,64,768]{2,1,0:T(8,128)(2,1)}), bf16[8,64,768]{2,1,0:T(8,128)(2,1)}, u32[]{:S(2)}, u32[]{:S(2)}) async-start(bf16[8,64,768]{2,1,0:T(8,128)(2,1)} %bitcast.492), calls=%async_computation.13 | async-start | bytes 1572864 | tf_op jit(solution)/shard_map/all_to_all | solution.py:373
  594.1 19.2 %all-to-all-start.10 = ((bf16[8,64,768]{2,1,0:T(8,128)(2,1)}), bf16[8,64,768]{2,1,0:T(8,128)(2,1)}, u32[]{:S(2)}, u32[]{:S(2)}) async-start(bf16[8,64,768]{2,1,0:T(8,128)(2,1)} %convolution_convert_fusion.8), calls=%async_computation.10 | async-start | bytes 1572864 | tf_op jit(solution)/shard_map/all_to_all | solution.py:354
  617.4 376.7 %reduce-scatter.5.cloned.1.call-start = ((), (), s32[]{:S(2)}) async-start(), calls=%async_computation.24 | async-start | bytes 5898240 | tf_op jit(solution)/shard_map/reduce_scatter | solution.py:423
  647.8 356.5 %reduce-scatter.11.cloned.1.call-start = ((), (), s32[]{:S(2)}) async-start(), calls=%async_computation.27 | async-start | bytes 5898240 | tf_op jit(solution)/shard_map/reduce_scatter | solution.py:416
  719.7 17.2 %all-to-all-start.15 = ((bf16[8,64,768]{2,1,0:T(8,128)(2,1)}), bf16[8,64,768]{2,1,0:T(8,128)(2,1)}, u32[]{:S(2)}, u32[]{:S(2)}) async-start(bf16[8,64,768]{2,1,0:T(8,128)(2,1)} %bitcast.113), calls=%async_computation.15 | async-start | bytes 1572864 | tf_op jit(solution)/shard_map/all_to_all | solution.py:373
  809.3 59.6 %all-to-all-start.17 = ((bf16[2,8,1152,128]{3,2,0,1:T(8,128)(2,1)}), bf16[2,8,1152,128]{3,2,0,1:T(8,128)(2,1)}, u32[]{:S(2)}, u32[]{:S(2)}) async-start(bf16[2,8,1152,128]{3,2,0,1:T(8,128)(2,1)} %copy.227), calls=%async_computation.17 | async-start | bytes 9437184 | tf_op jit(solution)/shard_map/all_to_all | solution.py:161
  868.9 59.4 %all-to-all-start.16 = ((bf16[2,8,1152,128]{3,2,0,1:T(8,128)(2,1)}), bf16[2,8,1152,128]{3,2,0,1:T(8,128)(2,1)}, u32[]{:S(2)}, u32[]{:S(2)}) async-start(bf16[2,8,1152,128]{3,2,0,1:T(8,128)(2,1)} %copy.224), calls=%async_computation.16 | async-start | bytes 9437184 | tf_op jit(solution)/shard_map/all_to_all | solution.py:161
  873.6 130.7 %reduce-scatter.9.cloned.1.call-start = ((), (), s32[]{:S(2)}) async-start(), calls=%async_computation.26 | async-start | bytes 5898240 | tf_op jit(solution)/shard_map/reduce_scatter | solution.py:416
  932.6 58.1 %all-to-all-start.19 = ((bf16[4,1168,128]{2,1,0:T(8,128)(2,1)}), bf16[4,1168,128]{2,1,0:T(8,128)(2,1)S(1)}, u32[]{:S(2)}, u32[]{:S(2)}) async-start(bf16[4,1168,128]{2,1,0:T(8,128)(2,1)} %pad_maximum_fusion.3), calls=%async_computation.19 | async-start | bytes 2392064 | tf_op jit(solution)/shard_map/all_to_all | solution.py:457
  (317 other events, 3520.6 us)
Sparse Core Ops, SparseCore 0:
  11.4 85.1 all-gather.10
  98.2 87.9 all-gather.12
  187.8 87.8 all-gather.14
  277.1 87.8 all-gather.16
  366.4 87.8 all-gather.18
  491.1 84.0 reduce-scatter.6
  647.9 82.1 reduce-scatter.4
  732.4 85.7 reduce-scatter.10
  882.6 102.3 reduce-scatter.8

commit v2 on v1

--- a/solution.py
+++ b/solution.py
@@ -150,14 +150,17 @@
     return pieces
 
 
-def dense_sums(grad_qkv, grad_out, dp_count, expert_lanes):
-    joined = jnp.concatenate(
+def dense_join(grad_qkv, grad_out, dp_count, expert_lanes):
+    return jnp.concatenate(
         [
             grad_qkv.astype(jnp.bfloat16).reshape(dp_count * expert_lanes, -1, 128),
             grad_out.astype(jnp.bfloat16).reshape(dp_count * expert_lanes, -1, 128),
         ],
         axis=1,
     ).reshape(dp_count, expert_lanes, -1, 128)
+
+
+def dense_exchange(joined):
     swapped = lax.all_to_all(joined, "expert", split_axis=1, concat_axis=1, tiled=True)
     return jnp.sum(swapped.astype(jnp.float32), axis=1)
 
@@ -313,8 +316,10 @@
     ein_parts = [None] * layer_count
     eout_parts = [None] * layer_count
     dense_parts = [None] * layer_count
+    waiting = None
     for layer_no in reversed(range(layer_count)):
         kept_hidden, kept_flat_grad, kept_rows, kept_inner = ([], [], [], [])
+        routed_grads = []
         kept_attended, kept_branch, kept_normed, kept_proj = ([], [], [], [])
         for batch_no in range(micro_count):
             grad_stream = grad_streams[batch_no]
@@ -380,6 +385,47 @@
             grad_normed_two = grad_normed_two + jnp.einsum(
                 "tec,ecd->td", slot_table, grad_back, preferred_element_type=jnp.float32
             )
+            routed_grads.append(grad_normed_two)
+        eout_full = jnp.einsum(
+            "rf,rd->fd",
+            jnp.concatenate(kept_hidden, axis=0),
+            jnp.concatenate(kept_flat_grad, axis=0),
+            preferred_element_type=jnp.float32,
+        ).astype(jnp.bfloat16)
+        ein_full = jnp.einsum(
+            "rf,rd->fd",
+            jnp.concatenate(kept_inner, axis=0),
+            jnp.concatenate(kept_rows, axis=0),
+            preferred_element_type=jnp.float32,
+        ).astype(jnp.bfloat16)
+        eout_parts[layer_no] = lax.psum_scatter(eout_full, "dp", scatter_dimension=0, tiled=True)
+        ein_full, routed_grads, waiting = lax.optimization_barrier(
+            (ein_full, routed_grads, waiting)
+        )
+        ein_parts[layer_no] = lax.psum_scatter(ein_full, "dp", scatter_dimension=0, tiled=True)
+        if waiting is not None:
+            dense_parts[layer_no + 1] = dense_exchange(waiting)
+        for batch_no in range(micro_count):
+            grad_stream = grad_streams[batch_no]
+            allowed = allowed_parts[batch_no]
+            gain_pair = full_gain[layer_no].astype(jnp.float32)
+            grad_normed_two = routed_grads[batch_no]
+            (
+                stream,
+                after_attn,
+                normed,
+                projected,
+                attended,
+                log_total,
+                normed_two,
+                chance,
+                onehot,
+                slot_table,
+                gate_value,
+                expert_mix,
+                arrived,
+                inner_act,
+            ) = saved[batch_no][layer_no]
             unit_two, recip_two = unit_scale(after_attn)
             grad_after, gain_two = norm_back(grad_normed_two, unit_two, recip_two, gain_pair[1])
             grad_after = grad_stream + grad_after
@@ -407,20 +453,6 @@
             grad_input, gain_one = norm_back(grad_normed, unit_one, recip_one, gain_pair[0])
             acc_gain[layer_no] = acc_gain[layer_no] + jnp.stack([gain_one, gain_two])
             grad_streams[batch_no] = grad_after + grad_input
-        eout_full = jnp.einsum(
-            "rf,rd->fd",
-            jnp.concatenate(kept_hidden, axis=0),
-            jnp.concatenate(kept_flat_grad, axis=0),
-            preferred_element_type=jnp.float32,
-        ).astype(jnp.bfloat16)
-        eout_parts[layer_no] = lax.psum_scatter(eout_full, "dp", scatter_dimension=0, tiled=True)
-        ein_full = jnp.einsum(
-            "rf,rd->fd",
-            jnp.concatenate(kept_inner, axis=0),
-            jnp.concatenate(kept_rows, axis=0),
-            preferred_element_type=jnp.float32,
-        ).astype(jnp.bfloat16)
-        ein_parts[layer_no] = lax.psum_scatter(ein_full, "dp", scatter_dimension=0, tiled=True)
         grad_out = jnp.einsum(
             "td,te->de",
             jnp.concatenate(kept_attended, axis=0),
@@ -433,9 +465,8 @@
             jnp.concatenate(kept_proj, axis=1),
             preferred_element_type=jnp.float32,
         )
-        dense_parts[layer_no] = dense_sums(
-            grad_qkv, grad_out, dp_count // layer_count, expert_lanes
-        )
+        waiting = dense_join(grad_qkv, grad_out, dp_count // layer_count, expert_lanes)
+    dense_parts[0] = dense_exchange(waiting)
     input_grad = jnp.concatenate(grad_streams, axis=0)
     small_pack = pack_small(
         (jnp.stack(acc_gain), jnp.stack(acc_table), jnp.stack(acc_router)), device_count

time: 1030 us -> 1060 us (1.029)
  blocking collectives: 0 us -> 15 us
  waiting for transfers between devices: 396 us -> 407 us
    all_to_all x4, waiting for transfers between devices: 26.6 us -> 7.99 us  [per_device(): lax.all_to_all(grad_rows.reshape(arrived_grad.shape), 'expert', split_axi...]
    all_gather x2, waiting for transfers between devices: 139 us -> 154 us  [per_device(): lax.all_gather(expert_out[layer_no], 'dp', axis=1, tiled=True)[0]]
    all_to_all x0 -> x1, blocking collectives: none -> 15 us  [per_device(): lax.all_to_all(grad_slots, 'expert', split_axis=0, concat_axis=0, tiled=T...]
    unnamed x626 -> x542, local copies, waits for them, and re-layouts: 25.9 us -> 27.3 us
  transfers between devices with their start and end apart: 29 -> 28, of which waited for: 19 -> 17; matrix products, arithmetic and copies ran while one was open for 48% -> 45% of each run, Pallas kernels for 0% -> 0%
where the time goes in v2:
time: 1060 us; the launch traced here: 1040 us
  waiting for transfers between devices  407 us (38%)
  matrix products  297 us (28%)
  local copies, waits for them, and re-layouts  156 us (15%)
  starting transfers between devices  80 us (8%)
  other arithmetic  72.6 us (7%)
  between operations  17.4 us (2%)
  blocking collectives  15 us (1%)
    all_gather x2, waiting for transfers between devices, per_device(): lax.all_gather(expert_out[layer_no], 'dp', axis=1, tiled=True)[0]  154 us
    all_to_all x2, waiting for transfers between devices, dense_exchange(): lax.all_to_all(joined, 'expert', split_axis=1, concat_axis=1, tiled=True)  84.9 us
    all_gather x1, waiting for transfers between devices, per_device(): every_pack = lax.all_gather(own_pack, ('dp', 'expert'), axis=0, tiled=False)  68.9 us
    all_to_all x1, waiting for transfers between devices, per_device(): lax.all_to_all(dense_pack, 'dp', split_axis=0, concat_axis=0, tiled=True)  43.1 us
    dot_general x4, matrix products, per_device(): jnp.dot(expert_flat_rows, weight_in, preferred_element_type=jnp.float32)  38.5 us
    dot_general x4, matrix products, per_device(): jnp.einsum('rd,fd->rf', flat_grad, weight_out, preferred_element_type=jnp...  36.1 us
    unnamed x542, local copies, waits for them, and re-layouts  27.3 us
    dot_general x4, matrix products, per_device(): jnp.einsum('rf,df->rd', grad_inner, weight_in, preferred_element_type=jnp...  26.7 us
  transfers between devices with their start and end apart: 28, of which 17 were waited for; matrix products, arithmetic and copies ran while one was open for 45% of the time, Pallas kernels for 0%

profile of v2, /device:TPU:0, one launch (start us, length us, event | category | flops | bytes accessed | tf_op | source)
XLA Modules:
  0.0 1044.5 jit_solution(15732462742234001009)
XLA Ops:
  28.0 68.9 %all-gather.11.cloned.1.call-done = bf16[37376,128]{1,0:T(8,128)(2,1)} async-done(((bf16[1168,128]{1,0:T(8,128)(2,1)}), bf16[37376,128]{1,0:T(8,128)(2,1)}) %all-gather.11.cloned.1.call-update) | async-done | bytes 9568272 | tf_op jit(solution)/shard_map/all_gather | solution.py:200
  186.5 10.3 multiply_convert_fusion.3
  196.7 79.2 %all-gather.15.cloned.1.call-done = bf16[1,1,3072,768]{3,2,1,0:T(8,128)(2,1)} async-done(((bf16[1,1,768,768]{3,2,1,0:T(8,128)(2,1)}), bf16[1,1,3072,768]{3,2,1,0:T(8,128)(2,1)}) %all-gather.15.cloned.1.call-update) | async-done | bytes 4718608 | tf_op jit(solution)/shard_map/all_gather | solution.py:216
  286.4 8.1 multiply_convert_fusion.1
  311.7 7.6 all-to-all-done.5
  356.7 8.5 all-gather.17.cloned.1.call-done
  365.2 10.2 multiply_convert_fusion
  379.7 74.8 %all-gather.19.cloned.1.call-done = bf16[1,1,3072,768]{3,2,1,0:T(8,128)(2,1)} async-done(((bf16[1,1,768,768]{3,2,1,0:T(8,128)(2,1)}), bf16[1,1,3072,768]{3,2,1,0:T(8,128)(2,1)}) %all-gather.19.cloned.1.call-update) | async-done | bytes 4718608 | tf_op jit(solution)/shard_map/all_gather | solution.py:216
  454.5 9.8 fusion.33
  468.8 9.9 multiply_convert_fusion.2
  481.4 8.7 fusion.19
  491.7 8.3 fusion.59
  511.2 9.3 fusion.50
  548.3 6.9 fusion.185
  635.8 12.0 %all-to-all-done.13 = bf16[8,64,768]{2,1,0:T(8,128)(2,1)S(1)} async-done(((bf16[8,64,768]{2,1,0:T(8,128)(2,1)}), bf16[8,64,768]{2,1,0:T(8,128)(2,1)S(1)}, u32[]{:S(2)}, u32[]{:S(2)}) %all-to-all-start.13) | async-done | bytes 786464 | tf_op jit(solution)/shard_map/all_to_all | solution.py:359
  647.8 15.0 %all_to_all.100 = bf16[8,64,768]{2,1,0:T(8,128)(2,1)S(1)} all-to-all(bf16[8,64,768]{2,1,0:T(8,128)(2,1)S(1)} %convolution_convert_fusion.7), channel_id=1, replica_groups=mesh['dp'=4,'expert'=8] {'expert'}, dimensions={0} | all-to-all | bytes 1572864 | tf_op jit(solution)/shard_map/all_to_all | solution.py:359
  663.6 8.6 fusion.53
  721.7 8.8 fusion.12
  730.5 7.0 fusion.170
  741.1 8.7 fusion.26
  762.1 9.8 fusion.56
  868.8 34.3 %all-to-all-done.17 = bf16[2,8,1152,128]{3,2,0,1:T(8,128)(2,1)} async-done(((bf16[2,8,1152,128]{3,2,0,1:T(8,128)(2,1)}), bf16[2,8,1152,128]{3,2,0,1:T(8,128)(2,1)}, u32[]{:S(2)}, u32[]{:S(2)}) %all-to-all-start.17) | async-done | bytes 4718624 | tf_op jit(solution)/shard_map/all_to_all | solution.py:164
  911.8 50.6 %all-to-all-done.16 = bf16[2,8,1152,128]{3,2,0,1:T(8,128)(2,1)} async-done(((bf16[2,8,1152,128]{3,2,0,1:T(8,128)(2,1)}), bf16[2,8,1152,128]{3,2,0,1:T(8,128)(2,1)}, u32[]{:S(2)}, u32[]{:S(2)}) %all-to-all-start.16) | async-done | bytes 4718624 | tf_op jit(solution)/shard_map/all_to_all | solution.py:164
  976.9 43.1 %all-to-all-done.19 = bf16[4,1168,128]{2,1,0:T(8,128)(2,1)S(1)} async-done(((bf16[4,1168,128]{2,1,0:T(8,128)(2,1)}), bf16[4,1168,128]{2,1,0:T(8,128)(2,1)S(1)}, u32[]{:S(2)}, u32[]{:S(2)}) %all-to-all-start.19) | async-done | bytes 1196064 | tf_op jit(solution)/shard_map/all_to_all | solution.py:488
  (874 shorter events, 508.7 us)
Async XLA Ops:
  7.2 89.7 %all-gather.11.cloned.1.call-start = ((), (), s32[]{:S(2)}) async-start(), calls=%async_computation.28 | async-start | bytes 9867264 | tf_op jit(solution)/shard_map/all_gather | solution.py:200
  10.4 176.1 %all-gather.13.cloned.1.call-start = ((), (), s32[]{:S(2)}) async-start(), calls=%async_computation.29 | async-start | bytes 5898240 | tf_op jit(solution)/shard_map/all_gather | solution.py:215
  13.9 262.1 %all-gather.15.cloned.1.call-start = ((), (), s32[]{:S(2)}) async-start(), calls=%async_computation.30 | async-start | bytes 5898240 | tf_op jit(solution)/shard_map/all_gather | solution.py:216
  15.6 349.7 %all-gather.17.cloned.1.call-start = ((), (), s32[]{:S(2)}) async-start(), calls=%async_computation.31 | async-start | bytes 5898240 | tf_op jit(solution)/shard_map/all_gather | solution.py:215
  16.1 438.4 %all-gather.19.cloned.1.call-start = ((), (), s32[]{:S(2)}) async-start(), calls=%async_computation.32 | async-start | bytes 5898240 | tf_op jit(solution)/shard_map/all_gather | solution.py:216
  152.1 24.8 %all-to-all-start = ((bf16[8,64,768]{2,1,0:T(8,128)(2,1)}), bf16[8,64,768]{2,1,0:T(8,128)(2,1)}, u32[]{:S(2)}, u32[]{:S(2)}) async-start(bf16[8,64,768]{2,1,0:T(8,128)(2,1)} %convolution_convert_fusion.13), calls=%async_computation | async-start | bytes 1572864 | tf_op jit(solution)/shard_map/all_to_all | solution.py:260
  177.0 105.7 %all-to-all-start.4 = ((bf16[8,64,768]{2,1,0:T(8,128)(2,1)}), bf16[8,64,768]{2,1,0:T(8,128)(2,1)S(1)}, u32[]{:S(2)}, u32[]{:S(2)}) async-start(bf16[8,64,768]{2,1,0:T(8,128)(2,1)} %convolution_convert_fusion.11), calls=%async_computation.4 | async-start | bytes 1572864 | tf_op jit(solution)/shard_map/all_to_all | solution.py:260
  282.7 19.3 %all-to-all-start.1 = ((bf16[8,64,768]{2,1,0:T(8,128)(2,1)}), bf16[8,64,768]{2,1,0:T(8,128)(2,1)S(1)}, u32[]{:S(2)}, u32[]{:S(2)}) async-start(bf16[8,64,768]{2,1,0:T(8,128)(2,1)} %bitcast.23), calls=%async_computation.1 | async-start | bytes 1572864 | tf_op jit(solution)/shard_map/all_to_all | solution.py:269
  302.0 17.2 %all-to-all-start.5 = ((bf16[8,64,768]{2,1,0:T(8,128)(2,1)}), bf16[8,64,768]{2,1,0:T(8,128)(2,1)}, u32[]{:S(2)}, u32[]{:S(2)}) async-start(bf16[8,64,768]{2,1,0:T(8,128)(2,1)} %bitcast.494), calls=%async_computation.5 | async-start | bytes 1572864 | tf_op jit(solution)/shard_map/all_to_all | solution.py:269
  335.3 16.8 %all-to-all-start.6 = ((bf16[8,64,768]{2,1,0:T(8,128)(2,1)}), bf16[8,64,768]{2,1,0:T(8,128)(2,1)}, u32[]{:S(2)}, u32[]{:S(2)}) async-start(bf16[8,64,768]{2,1,0:T(8,128)(2,1)} %convolution_convert_fusion.10), calls=%async_computation.6 | async-start | bytes 1572864 | tf_op jit(solution)/shard_map/all_to_all | solution.py:260
  352.1 23.4 %all-to-all-start.9 = ((bf16[8,64,768]{2,1,0:T(8,128)(2,1)}), bf16[8,64,768]{2,1,0:T(8,128)(2,1)}, u32[]{:S(2)}, u32[]{:S(2)}) async-start(bf16[8,64,768]{2,1,0:T(8,128)(2,1)} %convolution_convert_fusion.8), calls=%async_computation.9 | async-start | bytes 1572864 | tf_op jit(solution)/shard_map/all_to_all | solution.py:359
  375.5 88.9 %all-to-all-start.2 = ((bf16[8,64,768]{2,1,0:T(8,128)(2,1)}), bf16[8,64,768]{2,1,0:T(8,128)(2,1)}, u32[]{:S(2)}, u32[]{:S(2)}) async-start(bf16[8,64,768]{2,1,0:T(8,128)(2,1)} %convolution_convert_fusion.12), calls=%async_computation.2 | async-start | bytes 1572864 | tf_op jit(solution)/shard_map/all_to_all | solution.py:260
  464.4 17.0 %all-to-all-start.8 = ((bf16[8,64,768]{2,1,0:T(8,128)(2,1)}), bf16[8,64,768]{2,1,0:T(8,128)(2,1)}, u32[]{:S(2)}, u32[]{:S(2)}) async-start(bf16[8,64,768]{2,1,0:T(8,128)(2,1)} %convolution_convert_fusion.9), calls=%async_computation.8 | async-start | bytes 1572864 | tf_op jit(solution)/shard_map/all_to_all | solution.py:359
  506.9 20.4 %all-to-all-start.10 = ((bf16[8,64,768]{2,1,0:T(8,128)(2,1)}), bf16[8,64,768]{2,1,0:T(8,128)(2,1)}, u32[]{:S(2)}, u32[]{:S(2)}) async-start(bf16[8,64,768]{2,1,0:T(8,128)(2,1)} %bitcast.493), calls=%async_computation.10 | async-start | bytes 1572864 | tf_op jit(solution)/shard_map/all_to_all | solution.py:378
  511.1 512.3 %reduce-scatter.11.cloned.1.call-start = ((), (), s32[]{:S(2)}) async-start(), calls=%async_computation.27 | async-start | bytes 5898240 | tf_op jit(solution)/shard_map/reduce_scatter | solution.py:401
  527.3 16.8 %all-to-all-start.3 = ((bf16[8,64,768]{2,1,0:T(8,128)(2,1)}), bf16[8,64,768]{2,1,0:T(8,128)(2,1)}, u32[]{:S(2)}, u32[]{:S(2)}) async-start(bf16[8,64,768]{2,1,0:T(8,128)(2,1)} %bitcast.496), calls=%async_computation.3 | async-start | bytes 1572864 | tf_op jit(solution)/shard_map/all_to_all | solution.py:269
  635.2 388.2 %reduce-scatter.9.cloned.1.call-start = ((), (), s32[]{:S(2)}) async-start(), calls=%async_computation.26 | async-start | bytes 5898240 | tf_op jit(solution)/shard_map/reduce_scatter | solution.py:401
  672.3 355.2 %reduce-scatter.7.cloned.1.call-start = ((), (), s32[]{:S(2)}) async-start(), calls=%async_computation.25 | async-start | bytes 5898240 | tf_op jit(solution)/shard_map/reduce_scatter | solution.py:405
  737.5 19.9 %all-to-all-start.14 = ((bf16[8,64,768]{2,1,0:T(8,128)(2,1)}), bf16[8,64,768]{2,1,0:T(8,128)(2,1)S(1)}, u32[]{:S(2)}, u32[]{:S(2)}) async-start(bf16[8,64,768]{2,1,0:T(8,128)(2,1)} %bitcast.103), calls=%async_computation.14 | async-start | bytes 1572864 | tf_op jit(solution)/shard_map/all_to_all | solution.py:378
  757.4 17.2 %all-to-all-start.15 = ((bf16[8,64,768]{2,1,0:T(8,128)(2,1)}), bf16[8,64,768]{2,1,0:T(8,128)(2,1)}, u32[]{:S(2)}, u32[]{:S(2)}) async-start(bf16[8,64,768]{2,1,0:T(8,128)(2,1)} %bitcast.105), calls=%async_computation.15 | async-start | bytes 1572864 | tf_op jit(solution)/shard_map/all_to_all | solution.py:378
  843.5 59.6 %all-to-all-start.17 = ((bf16[2,8,1152,128]{3,2,0,1:T(8,128)(2,1)}), bf16[2,8,1152,128]{3,2,0,1:T(8,128)(2,1)}, u32[]{:S(2)}, u32[]{:S(2)}) async-start(bf16[2,8,1152,128]{3,2,0,1:T(8,128)(2,1)} %copy.227), calls=%async_computation.17 | async-start | bytes 9437184 | tf_op jit(solution)/shard_map/all_to_all | solution.py:164
  903.1 59.4 %all-to-all-start.16 = ((bf16[2,8,1152,128]{3,2,0,1:T(8,128)(2,1)}), bf16[2,8,1152,128]{3,2,0,1:T(8,128)(2,1)}, u32[]{:S(2)}, u32[]{:S(2)}) async-start(bf16[2,8,1152,128]{3,2,0,1:T(8,128)(2,1)} %copy.226), calls=%async_computation.16 | async-start | bytes 9437184 | tf_op jit(solution)/shard_map/all_to_all | solution.py:164
  907.7 119.8 %reduce-scatter.5.cloned.1.call-start = ((), (), s32[]{:S(2)}) async-start(), calls=%async_computation.24 | async-start | bytes 5898240 | tf_op jit(solution)/shard_map/reduce_scatter | solution.py:405
  966.8 53.3 %all-to-all-start.19 = ((bf16[4,1168,128]{2,1,0:T(8,128)(2,1)}), bf16[4,1168,128]{2,1,0:T(8,128)(2,1)S(1)}, u32[]{:S(2)}, u32[]{:S(2)}) async-start(bf16[4,1168,128]{2,1,0:T(8,128)(2,1)} %pad_maximum_fusion.3), calls=%async_computation.19 | async-start | bytes 2392064 | tf_op jit(solution)/shard_map/all_to_all | solution.py:488
  (274 other events, 2529.0 us)
Sparse Core Ops, SparseCore 0:
  11.4 85.3 all-gather.10
  98.4 87.9 all-gather.12
  188.1 87.8 all-gather.14
  277.3 87.8 all-gather.16
  366.7 87.8 all-gather.18
  520.6 84.0 reduce-scatter.10
  672.4 81.7 reduce-scatter.8
  756.5 85.7 reduce-scatter.6
  910.8 101.8 reduce-scatter.4
